TPU v7x, 32 devices: a whole 2x2x4 slice. The times are simulated.
32 devices in a mesh: frame: 8 (over y, x, core), space: 4 (over z).
Axes of the slice: x: 2, y: 2, z: 4, core: 2. Of those that a mesh axis runs over, the one named last changes fastest.
Arguments:
- query_tokens: bfloat16 [8, 1024, 2240], P('frame', 'space'), may hold values from -6 to 6
- key_tokens: bfloat16 [8, 1024, 2240], P('frame', 'space'), may hold values from -500 to 500
- value_tokens: bfloat16 [8, 1024, 2240], P('frame', 'space'), may hold values from -6 to 6
- out_grad: bfloat16 [8, 1024, 2240], P('frame', 'space'), may hold values from -768 to 768
Outputs:
- query_grad: float32 [8, 1024, 2240], P('frame', 'space')
- key_grad: float32 [8, 1024, 2240], P('frame', 'space')
- value_grad: float32 [8, 1024, 2240], P('frame', 'space')
All inputs are finite; a program needn't handle non-finite values.
Results may differ from a plain program's by a relative error of at most 0.0041.
Values sent between devices are 32-bit elements; how exact they have to be, the bound alone decides.
A program may use at most 128 MiB of HBM per device.

v0:
```python
import jax
import jax.numpy as jnp
from jax import lax
from jax.sharding import PartitionSpec as P

HEADS = 20
HEAD_DIM = 112


HIGH = lax.Precision.HIGHEST


def entering(array, axis, combine, identity, reverse):
    devices, position = (lax.axis_size(axis), lax.axis_index(axis))
    everything = jax.tree.map(lambda part: lax.all_gather(part, axis), array)
    start = jax.tree.map(
        lambda part, zero: jnp.broadcast_to(jnp.asarray(zero, part.dtype), part.shape),
        array,
        identity,
    )

    def lap(k, before):
        at = devices - 1 - k if reverse else k
        reached = at > position if reverse else at < position
        new = combine(before, jax.tree.map(lambda part: part[at], everything))
        return jax.tree.map(lambda a, b: jnp.where(reached, a, b), new, before)

    return lax.fori_loop(0, devices, lap, start)


def add_pair(earlier, later):
    return (earlier[0] + later[0], earlier[1] + later[1])


def prefix_states(local_state, local_z):
    totals = lax.psum((local_state, local_z), "space")
    blank = (jnp.zeros_like(totals[0]), jnp.zeros_like(totals[1]))
    before = entering(totals, "frame", add_pair, blank, False)
    return add_pair(before, totals)


def suffix_grads(local_grad, local_zgrad):
    totals = lax.psum((local_grad, local_zgrad), "space")
    blank = (jnp.zeros_like(totals[0]), jnp.zeros_like(totals[1]))
    after = entering(totals, "frame", add_pair, blank, True)
    return add_pair(after, totals)


def on_device(query_tokens, key_tokens, value_tokens, out_grad):
    tile_rows = query_tokens.shape[1]
    q_heads = query_tokens.reshape(tile_rows, HEADS, HEAD_DIM)
    k_heads = key_tokens.reshape(tile_rows, HEADS, HEAD_DIM)
    v_heads = value_tokens.reshape(tile_rows, HEADS, HEAD_DIM)
    q_feat = jnp.maximum(q_heads, 0)
    k_feat = jnp.maximum(k_heads, 0)
    local_state = jnp.einsum("thi,thj->ihj", k_feat, v_heads, preferred_element_type=jnp.float32)
    local_z = jnp.sum(k_feat, axis=0, dtype=jnp.float32).T
    state_flat, zsum = prefix_states(local_state.reshape(HEAD_DIM, HEADS * HEAD_DIM), local_z)
    state = state_flat.reshape(HEAD_DIM, HEADS, HEAD_DIM)
    q_wide = q_feat.astype(jnp.float32)
    out_heads = out_grad.reshape(tile_rows, HEADS, HEAD_DIM).astype(jnp.float32)
    numerator = jnp.einsum("thi,ihj->thj", q_wide, state, precision=HIGH)
    denominator = jnp.einsum("thi,ih->th", q_wide, zsum, precision=HIGH) + 1.0
    scaled_low = (out_heads / denominator[:, :, None]).astype(jnp.bfloat16)
    scaled = lax.optimization_barrier(scaled_low).astype(jnp.float32)
    denom_grad = -jnp.sum(out_heads * numerator, axis=-1) / (denominator * denominator)
    direct = jnp.einsum("thj,ihj->thi", scaled, state, precision=HIGH)
    query_grad = jnp.where(q_heads > 0, direct + denom_grad[:, :, None] * zsum.T[None], 0.0)
    local_grad = jnp.einsum("thi,thj->ihj", q_feat, scaled_low, preferred_element_type=jnp.float32)
    local_zgrad = jnp.einsum("thi,th->ih", q_wide, denom_grad, precision=HIGH)
    grad_flat, zsum_grad = suffix_grads(local_grad.reshape(HEAD_DIM, HEADS * HEAD_DIM), local_zgrad)
    state_grad = grad_flat.reshape(HEAD_DIM, HEADS, HEAD_DIM)
    k_wide = k_feat.astype(jnp.float32)
    v_wide = v_heads.astype(jnp.float32)
    value_grad = jnp.einsum("thi,ihj->thj", k_wide, state_grad, precision=HIGH)
    key_part = jnp.einsum("thj,ihj->thi", v_wide, state_grad, precision=HIGH)
    key_grad = jnp.where(k_heads > 0, key_part + zsum_grad.T[None], 0.0)
    width_all = HEADS * HEAD_DIM
    return (
        query_grad.reshape(1, tile_rows, width_all),
        key_grad.reshape(1, tile_rows, width_all),
        value_grad.reshape(1, tile_rows, width_all),
    )


def solution(mesh):
    placed = (
        P("frame", "space", None),
        P("frame", "space", None),
        P("frame", "space", None),
        P("frame", "space", None),
    )
    return jax.shard_map(
        on_device,
        mesh=mesh,
        in_specs=placed,
        out_specs=(P("frame", "space", None), P("frame", "space", None), P("frame", "space", None)),
        check_vma=False,
    )
```

profile of v0, /device:TPU:0, one launch (start us, length us, event | category | flops | bytes accessed | tf_op | source)
XLA Modules:
  0.0 278.3 jit_solution(2375803570704088883)
XLA Ops:
  11.6 57.7 %all-reduce.3.cloned.1.call-done = f32[112,2240]{0,1:T(8,128)} async-done(((f32[112,2240]{0,1:T(8,128)}), f32[112,2240]{0,1:T(8,128)}) %all-reduce.3.cloned.1.call-update) | async-done | bytes 1003536 | tf_op jit(solution)/shard_map/psum | solution.py:36
  69.3 2.6 copy.27
  72.5 17.2 %psum.29 = f32[112,20]{0,1:T(8,128)S(1)} all-reduce(f32[112,20]{0,1:T(8,128)S(1)} %bitcast.111), channel_id=1, replica_groups=mesh['frame'=8,'space'=4] {'space'}, use_global_device_ids=true, to_apply=%region_2.0 | all-reduce | flops 2240 | bytes 17920 | tf_op jit(solution)/shard_map/psum | solution.py:36
  89.7 9.2 %all-gather.4 = f32[8,112,20]{1,2,0:T(8,128)S(1)} all-gather(f32[1,112,20]{1,2,0:T(8,128)S(1)} %bitcast.110), channel_id=3, replica_groups=mesh['frame'=8,'space'=4] {'frame'}, dimensions={0}, use_global_device_ids=true | all-gather | bytes 80640 | tf_op jit(solution)/shard_map/all_gather | solution.py:15
  98.9 1.7 broadcast_maximum_fusion
  100.6 25.1 %all-gather.9.cloned.1.call-done = f32[896,2240]{1,0:T(8,128)} async-done(((f32[112,2240]{1,0:T(8,128)}), f32[896,2240]{1,0:T(8,128)}) %all-gather.9.cloned.1.call-update) | async-done | bytes 8028176 | tf_op jit(solution)/shard_map/all_gather | solution.py:15
  125.7 12.5 %while.34 = (s32[]{:T(128)}, f32[112,2240]{1,0:T(8,128)S(1)}, f32[112,20]{0,1:T(8,128)S(1)}, s32[]{:T(128)}, f32[8,112,2240]{2,1,0:T(8,128)}, /*index=5*/f32[8,112,20]{1,2,0:T(8,128)S(1)}, s32[]{:T(128)}, s32[]{:T(128)}) while((s32[]{:T(128)}, f32[112,2240]{1,0:T(8,128)S(1)}, f32[112,20]{0,1:T(8,128)S(1)}, s32[]{:T(128)}, ...), condition=%wide.region_4.5_spmd.clone, body=%wide.region_3.4_spmd.clone.sunk | while | flops 759364 | bytes 3037555 | solution.py:28
  141.3 2.6 copy.30
  143.9 51.7 %all-reduce.5.cloned.1.call-done = f32[112,2240]{1,0:T(8,128)} async-done(((f32[112,2240]{1,0:T(8,128)}), f32[112,2240]{1,0:T(8,128)}) %all-reduce.5.cloned.1.call-update) | async-done | bytes 1003536 | tf_op jit(solution)/shard_map/psum | solution.py:43
  195.7 2.5 broadcast_compare_fusion
  200.7 1.9 add.130
  205.3 17.0 %psum.31 = f32[112,20]{0,1:T(8,128)S(1)} all-reduce(f32[112,20]{0,1:T(8,128)S(1)} %bitcast.112), channel_id=1, replica_groups=mesh['frame'=8,'space'=4] {'space'}, use_global_device_ids=true, to_apply=%region_7.8 | all-reduce | flops 2240 | bytes 17920 | tf_op jit(solution)/shard_map/psum | solution.py:43
  222.3 9.5 %all-gather.5 = f32[8,112,20]{1,2,0:T(8,128)S(1)} all-gather(f32[1,112,20]{1,2,0:T(8,128)S(1)} %bitcast.109), channel_id=5, replica_groups=mesh['frame'=8,'space'=4] {'frame'}, dimensions={0}, use_global_device_ids=true | all-gather | bytes 80640 | tf_op jit(solution)/shard_map/all_gather | solution.py:15
  231.8 4.4 %fusion.2 = f32[256,20,112]{0,2,1:T(8,128)} fusion(pred[256,20,112]{0,2,1:T(8,128)(4,1)S(1)} %bitcast.104, f32[112,20,112]{0,2,1:T(8,128)} %bitcast.94, bf16[256,20,112]{0,2,1:T(8,128)(2,1)} %copy-done.6, f32[20,112]{1,0:T(8,128)S(1)} %get-tuple-element.350, f32[256,20]{0,1:T(8,128)S(1)} %multiply_divide_fusion), kind=kOutput, calls=%fused_computation.10 | convolution fusion | flops 772423680 | bytes 5047040 | tf_op jit(solution)/shard_map/thj,ihj->thi/dot_general | solution.py:67
  236.2 14.8 %all-gather.11.cloned.1.call-done = f32[896,2240]{1,0:T(8,128)} async-done(((f32[112,2240]{1,0:T(8,128)}), f32[896,2240]{1,0:T(8,128)}) %all-gather.11.cloned.1.call-update) | async-done | bytes 8028176 | tf_op jit(solution)/shard_map/all_gather | solution.py:15
  251.1 12.6 %while.35 = (s32[]{:T(128)}, f32[112,2240]{1,0:T(8,128)S(1)}, f32[112,20]{0,1:T(8,128)S(1)}, s32[]{:T(128)}, f32[8,112,2240]{2,1,0:T(8,128)}, /*index=5*/f32[8,1...) while((s32[]{:T(128)}, f32[112,2240]{1,0:T(8,128)S(1)}, ...), condition=%wide.region_9.10_spmd.clone, body=%wide.region_8.9_spmd.clone.sunk | while | flops 759368 | bytes 3037617 | solution.py:28
  251.1 1.6 add_select_fusion.10
  252.7 1.5 add_select_fusion.10
  254.3 1.5 add_select_fusion.10
  255.9 1.5 add_select_fusion.10
  259.0 1.5 add_select_fusion.10
  264.8 1.7 copy.31
  266.5 2.4 fusion.9
  268.9 2.8 %bitcast_select_fusion = f32[256,20,112]{0,2,1:T(8,128)} fusion(pred[256,20,112]{0,2,1:T(8,128)(4,1)S(1)} %bitcast.103, f32[112,20,112]{0,2,1:T(8,128)S(1)} %bitcast.96, bf16[256,20,112]{0,2,1:T(8,128)(2,1)S(1)} %bitcast.86, f32[20,112]{1,0:T(8,128)S(1)} %add_bitcast_fusion), kind=kOutput, calls=%fused_computation.8 | convolution fusion | flops 771850240 | bytes 5026560 | tf_op jit(solution)/shard_map/thj,ihj->thi/dot_general | solution.py:76
  (85 shorter events, 31.3 us)
Async XLA Ops:
  7.2 1.6 copy-start
  7.2 62.1 %all-reduce.3.cloned.1.call-start = ((), (), s32[]{:S(2)}) async-start(), calls=%async_computation | async-start | bytes 2293760 | tf_op jit(solution)/shard_map/psum | solution.py:36
  8.6 1.1 copy-start.4
  11.6 60.4 %copy-start.3 = (bf16[1,256,2240]{1,2,0:T(8,128)(2,1)S(1)}, bf16[1,256,2240]{1,2,0:T(8,128)(2,1)}, u32[]{:S(2)}) copy-start(bf16[1,256,2240]{1,2,0:T(8,128)(2,1)} %param.9) | copy-start | bytes 3440644
  11.6 114.1 %all-gather.9.cloned.1.call-start = ((), (), s32[]{:S(2)}) async-start(), calls=%async_computation.2 | async-start | bytes 9289728 | tf_op jit(solution)/shard_map/all_gather | solution.py:15
  71.9 123.7 %all-reduce.5.cloned.1.call-start = ((), (), s32[]{:S(2)}) async-start(), calls=%async_computation.1 | async-start | bytes 2064384 | tf_op jit(solution)/shard_map/psum | solution.py:43
  100.6 39.2 %copy-start.1 = (bf16[1,256,2240]{1,2,0:T(8,128)(2,1)}, bf16[1,256,2240]{1,2,0:T(8,128)(2,1)S(1)}, u32[]{:S(2)}) copy-start(bf16[1,256,2240]{1,2,0:T(8,128)(2,1)S(1)} %broadcast_maximum_fusion) | copy-start | bytes 3440644
  138.2 1.3 copy-start.9
  139.8 1.5 copy-start.6
  143.9 107.2 %all-gather.11.cloned.1.call-start = ((), (), s32[]{:S(2)}) async-start(), calls=%async_computation.3 | async-start | bytes 9289728 | tf_op jit(solution)/shard_map/all_gather | solution.py:15
  195.7 2.5 copy-start.8
  200.7 1.9 copy-start.2
  200.7 2.3 copy-start.10
  202.6 1.7 copy-start.7
  204.3 27.5 %copy-start.13 = (pred[1,256,2240]{1,2,0:T(8,128)(4,1)S(1)}, pred[1,256,2240]{1,2,0:T(8,128)(4,1)}, u32[]{:S(2)}) copy-start(pred[1,256,2240]{1,2,0:T(8,128)(4,1)} %broadcast_compare_fusion.1) | copy-start | bytes 1720324
  251.1 12.7 %copy-start.11 = (f32[112,2240]{1,0:T(8,128)S(1)}, f32[112,2240]{1,0:T(8,128)}, u32[]{:S(2)}) copy-start(f32[112,2240]{1,0:T(8,128)} %all-reduce.5.cloned.1.call-done) | copy-start | bytes 3010564
  264.8 1.7 copy-start.5
  266.5 2.4 copy-start.12
Sparse Core Ops, SparseCore 0:
  11.7 57.5 all-reduce.2
  72.1 53.5 all-gather.8
  144.0 51.5 all-reduce.4
  197.5 53.4 all-gather.10
where the time goes:
time: 279 us; the launch traced here: 278 us
  waiting for transfers between devices  149 us (53%)
  blocking collectives  52.9 us (19%)
  other arithmetic  35 us (13%)
  matrix products  14.4 us (5%)
  between operations  14 us (5%)
  local copies, waits for them, and re-layouts  11.9 us (4%)
    psum x1, waiting for transfers between devices, prefix_states(): totals = lax.psum((local_state, local_z), 'space')  57.7 us
    psum x1, waiting for transfers between devices, suffix_grads(): totals = lax.psum((local_grad, local_zgrad), 'space')  51.7 us
    all_gather x2, waiting for transfers between devices, entering(): everything = jax.tree.map(lambda part: lax.all_gather(part, axis), array)  39.9 us
    select_n x32, other arithmetic, lap(): return jax.tree.map(lambda a, b: jnp.where(reached, a, b), new, before)  24.6 us
    all_gather x2, blocking collectives, entering(): everything = jax.tree.map(lambda part: lax.all_gather(part, axis), array)  18.7 us
    psum x1, blocking collectives, prefix_states(): totals = lax.psum((local_state, local_z), 'space')  17.2 us
    psum x1, blocking collectives, suffix_grads(): totals = lax.psum((local_grad, local_zgrad), 'space')  17 us
  transfers between devices with their start and end apart: 4, of which 4 were waited for; matrix products, arithmetic and copies ran while one was open for 6% of the time, Pallas kernels for 0%

commit v1 on v0

v1 whole, which is shorter than its diff:
```python
import functools

import jax
import jax.numpy as jnp
from jax import lax
from jax.experimental import pallas as pl
from jax.experimental.pallas import tpu as pltpu
from jax.sharding import PartitionSpec as P

HEADS = 20
HEAD_DIM = 112
LANES = 128
MESH = pl.DeviceIdType.MESH
NT = (((1,), (1,)), ((), ()))
TN = (((0,), (0,)), ((), ()))


def dot(a, b, dims=(((1,), (0,)), ((), ()))):
    return lax.dot_general(a, b, dims, preferred_element_type=jnp.float32)


def split(state):
    high = state.astype(jnp.bfloat16)
    low = (state - high.astype(jnp.float32)).astype(jnp.bfloat16)
    return jnp.concatenate([high, low], axis=1)


def twice(a):
    return jnp.concatenate([a, a], axis=1)


def kernel(
    n_frame, n_space,
    q_ref, k_ref, v_ref, g_ref,
    oq_ref, ok_ref, ov_ref,
    qs, ks, vs, gs, sq, sk, sv,
    local, prefix, total, arrived, send_sem, recv_sem,
):
    frame, space = lax.axis_index("frame"), lax.axis_index("space")
    levels = max(n_frame - 1, 0).bit_length()
    hops = levels + n_space - 1
    right_link, left_link = levels, levels + 1

    def place(phase):
        return frame if phase == 0 else n_frame - 1 - frame

    def partner(phase, level):
        at = place(phase)
        other = at ^ (1 << level)
        upper = lax.rem(at // (1 << level), 2) == 1
        exists = other < n_frame
        sends, receives = exists, exists
        if level == levels - 1:
            sends = jnp.logical_and(exists, jnp.logical_not(upper))
            receives = jnp.logical_and(exists, upper)
        return other if phase == 0 else n_frame - 1 - other, upper, exists, sends, receives

    def link(phase, number, h, source):
        if number == right_link:
            device = (frame, space + 1)
        elif number == left_link:
            device = (frame, space - 1)
        else:
            device = (partner(phase, number)[0], space)
        return pltpu.make_async_remote_copy(
            src_ref=source,
            dst_ref=arrived.at[phase, number, h],
            send_sem=send_sem.at[phase, number, h],
            recv_sem=recv_sem.at[phase, number, h],
            device_id=device,
            device_id_type=MESH,
        )

    barrier = pltpu.get_barrier_semaphore()
    greet = [(space + 1 < n_space, (frame, space + 1)), (space > 0, (frame, space - 1))]
    for phase in (0,) if n_frame & (n_frame - 1) == 0 else (0, 1):
        for level in range(levels):
            other, _, exists, _, _ = partner(phase, level)
            greet.append((exists, (other, space)))
    for exists, device in greet:
        @pl.when(exists)
        def _(device=device):
            pl.semaphore_signal(barrier, inc=1, device_id=device, device_id_type=MESH)

    rows = q_ref.shape[1]
    lane = lax.broadcasted_iota(jnp.int32, (rows, LANES), 1)
    extra = jnp.logical_or(lane == HEAD_DIM, lane == HEAD_DIM + 1)
    pad = jnp.zeros((rows, LANES - HEAD_DIM), jnp.bfloat16)
    ones = jnp.where(extra, 1.0, 0.0).astype(jnp.bfloat16)[:, HEAD_DIM:]
    for h in range(HEADS):
        cut = slice(h * HEAD_DIM, (h + 1) * HEAD_DIM)
        ks[h] = jnp.concatenate([jnp.maximum(k_ref[0, :, cut], 0), pad], axis=1)
        vs[h] = jnp.concatenate([v_ref[0, :, cut], ones], axis=1)
        qs[h] = jnp.concatenate([jnp.maximum(q_ref[0, :, cut], 0), pad], axis=1)
        gs[h] = jnp.concatenate([g_ref[0, :, cut], pad], axis=1)

    pl.semaphore_wait(barrier, sum(jnp.int32(exists) for exists, _ in greet))

    def begin(phase, h, value):
        local[phase, h] = value
        prefix[phase, h] = value
        if levels:
            sends = partner(phase, 0)[3]

            @pl.when(sends)
            def _():
                link(phase, 0, h, local.at[phase, h]).start()

    def scan_level(phase, level, h):
        _, upper, exists, sends, receives = partner(phase, level)
        source = local.at[phase, h] if level == 0 else arrived.at[phase, level - 1, h]

        @pl.when(receives)
        def _():
            link(phase, level, h, source).wait_recv()
            came = arrived[phase, level, h]

            @pl.when(upper)
            def _():
                prefix[phase, h] = prefix[phase, h] + came

            if level + 1 < levels:
                arrived[phase, level, h] = came + source[...]

        if level + 1 < levels:
            follows = partner(phase, level + 1)[3]

            @pl.when(follows)
            def _():
                link(phase, level + 1, h, arrived.at[phase, level, h]).start()

        if level + 1 == levels:
            begin_chain(phase, h)

    def begin_chain(phase, h):
        own = prefix.at[phase, h]
        total[phase, h] = own[...]
        if n_space > 1:
            @pl.when(space == 0)
            def _():
                link(phase, right_link, h, own).start()

            @pl.when(space == n_space - 1)
            def _():
                link(phase, left_link, h, own).start()

    def chain_hop(phase, hop, h):
        for number, at in ((right_link, space), (left_link, n_space - 1 - space)):
            @pl.when(at == hop)
            def _(number=number):
                slot = arrived.at[phase, number, h]
                link(phase, number, h, slot).wait_recv()
                came = slot[...]
                total[phase, h] = total[phase, h] + came
                if hop < n_space - 1:
                    slot[...] = came + prefix[phase, h]
                    link(phase, number, h, slot).start()

    def states(h):
        begin(0, h, dot(ks[h][:, :HEAD_DIM], vs[h], TN))

    def queries(h):
        q = qs[h][:, :HEAD_DIM]
        both = split(total[0, h])
        wide = dot(q, both)
        numerator = wide[:, :LANES] + wide[:, LANES:]
        denominator = numerator[:, HEAD_DIM:HEAD_DIM + 1] + 1.0
        grad = gs[h].astype(jnp.float32)
        slope = -jnp.sum(grad * numerator, axis=1, keepdims=True) / (denominator * denominator)
        coarse = slope.astype(jnp.bfloat16).astype(jnp.float32)
        scaled = jnp.where(lane == HEAD_DIM, coarse,
                           jnp.where(lane == HEAD_DIM + 1, slope - coarse, grad / denominator))
        scaled = scaled.astype(jnp.bfloat16)
        begin(1, h, dot(q, scaled, TN))
        back = dot(twice(scaled), both, NT)
        sq[h, :, :HEAD_DIM] = jnp.where(q.astype(jnp.float32) > 0, back, 0.0)

    def keys(h):
        k = ks[h][:, :HEAD_DIM]
        both = split(total[1, h])
        wide = dot(k, both)
        sv[h] = wide[:, :LANES] + wide[:, LANES:]
        back = dot(twice(vs[h]), both, NT)
        sk[h, :, :HEAD_DIM] = jnp.where(k.astype(jnp.float32) > 0, back, 0.0)

    def stage(t, lag, act):
        h = t - lag

        @pl.when(jnp.logical_and(h >= 0, h < HEADS))
        def _():
            act(h)

    def step(t, carry):
        for phase in (1, 0):
            for hop in range(n_space - 1, 0, -1):
                stage(t, phase * hops + levels + hop, functools.partial(chain_hop, phase, hop))
            for level in range(levels - 1, -1, -1):
                stage(t, phase * hops + level + 1, functools.partial(scan_level, phase, level))
        stage(t, 0, states)
        stage(t, hops, queries)
        stage(t, 2 * hops, keys)
        return carry

    lax.fori_loop(0, HEADS + 2 * hops, step, 0)

    for h in range(HEADS):
        cut = slice(h * HEAD_DIM, (h + 1) * HEAD_DIM)
        oq_ref[0, :, cut] = sq[h, :, :HEAD_DIM]
        ok_ref[0, :, cut] = sk[h, :, :HEAD_DIM]
        ov_ref[0, :, cut] = sv[h, :, :HEAD_DIM]

    def drain(h, carry):
        for phase in (0, 1):
            for level in range(levels):
                source = local.at[phase, h] if level == 0 else arrived.at[phase, level - 1, h]

                @pl.when(partner(phase, level)[3])
                def _(source=source, level=level):
                    link(phase, level, h, source).wait_send()
            for number, sends in ((right_link, space < n_space - 1), (left_link, space > 0)):
                @pl.when(sends)
                def _(number=number):
                    link(phase, number, h, prefix.at[phase, h]).wait_send()
        return carry

    lax.fori_loop(0, HEADS, drain, 0)


def on_device(n_frame, n_space, query_tokens, key_tokens, value_tokens, out_grad):
    shape = query_tokens.shape
    rows = shape[1]
    levels = max(n_frame - 1, 0).bit_length()
    out = jax.ShapeDtypeStruct(shape, jnp.float32)
    tokens = pltpu.VMEM((HEADS, rows, LANES), jnp.bfloat16)
    results = pltpu.VMEM((HEADS, rows, LANES), jnp.float32)
    state = (HEADS, HEAD_DIM, LANES)
    links = (2, levels + 2, HEADS)
    return pl.pallas_call(
        functools.partial(kernel, n_frame, n_space),
        out_shape=(out, out, out),
        in_specs=[pl.BlockSpec(memory_space=pltpu.VMEM)] * 4,
        out_specs=(pl.BlockSpec(memory_space=pltpu.VMEM),) * 3,
        scratch_shapes=[tokens] * 4 + [results] * 3 + [pltpu.VMEM((2,) + state, jnp.float32)] * 3 + [
            pltpu.VMEM((2, levels + 2) + state, jnp.float32),
            pltpu.SemaphoreType.DMA(links),
            pltpu.SemaphoreType.DMA(links),
        ],
        compiler_params=pltpu.CompilerParams(
            collective_id=0, has_side_effects=True, vmem_limit_bytes=60 * 1024 * 1024
        ),
    )(query_tokens, key_tokens, value_tokens, out_grad)


def solution(mesh):
    placed = P("frame", "space", None)
    return jax.shard_map(
        functools.partial(on_device, mesh.shape["frame"], mesh.shape["space"]),
        mesh=mesh,
        in_specs=(placed,) * 4,
        out_specs=(placed,) * 3,
        check_vma=False,
    )
```

time: 279 us -> 135 us (0.48)
  waiting for transfers between devices: 149 us -> 0 us
  Pallas kernels: 0 us -> 119 us
  blocking collectives: 52.9 us -> 0 us
  other arithmetic: 35 us -> 0 us
  matrix products: 14.4 us -> 0 us
  between operations: 14 us -> 0.65 us
  local copies, waits for them, and re-layouts: 11.9 us -> 15.2 us
    pallas_call x0 -> x1, Pallas kernels: none -> 119 us  [on_device(): pl.pallas_call(functools.partial(kernel, n_frame, n_space), out_shape=(ou...]
    psum x2 -> x0, waiting for transfers between devices: 109 us -> none  [the longest x1 57.7 us: prefix_states(): totals = lax.psum((local_state, local_z), 'space')]
    all_gather x2 -> x0, waiting for transfers between devices: 39.9 us -> none  [entering(): everything = jax.tree.map(lambda part: lax.all_gather(part, axis), array)]
    psum x2 -> x0, blocking collectives: 34.2 us -> none  [the longest x1 17.2 us: prefix_states(): totals = lax.psum((local_state, local_z), 'space')]
    select_n x32 -> x0, other arithmetic: 24.6 us -> none  [lap(): return jax.tree.map(lambda a, b: jnp.where(reached, a, b), new, before)]
    all_gather x2 -> x0, blocking collectives: 18.7 us -> none  [entering(): everything = jax.tree.map(lambda part: lax.all_gather(part, axis), array)]
    dot_general x8 -> x0, matrix products: 14.4 us -> none  [the longest x1 4.42 us: on_device(): direct = jnp.einsum('thj,ihj->thi', scaled, state, precision=HIGH)]
    pallas_call x0 -> x3, local copies, waits for them, and re-layouts: none -> 8.12 us  [on_device(): pl.pallas_call(functools.partial(kernel, n_frame, n_space), out_shape=(ou...]
  transfers between devices with their start and end apart: 4 -> 0, of which waited for: 4 -> 0; matrix products, arithmetic and copies ran while one was open for 6% -> 0% of each run, Pallas kernels for 0% -> 0%
where the time goes in v1:
time: 135 us
  Pallas kernels  119 us (88%)
  local copies, waits for them, and re-layouts  15.2 us (11%)
    pallas_call x1, Pallas kernels, on_device(): pl.pallas_call(functools.partial(kernel, n_frame, n_space), out_shape=(ou...  119 us
    pallas_call x3, local copies, waits for them, and re-layouts, on_device(): pl.pallas_call(functools.partial(kernel, n_frame, n_space), out_shape=(ou...  8.12 us
    unnamed x12, local copies, waits for them, and re-layouts  7.05 us

profile of v1, /device:TPU:0, one launch (start us, length us, event | category | flops | bytes accessed | tf_op | source)
XLA Modules:
  0.0 134.9 jit_solution(14858536246690615763)
XLA Ops:
  0.6 0.0 copy-start.1
  0.6 2.5 %copy.7.q_ref = bf16[1,256,2240]{2,1,0:T(8,128)(2,1)} copy(bf16[1,256,2240]{1,2,0:T(8,128)(2,1)} %param.4) | data formatting | bytes 2293760 | tf_op args[0]
  3.1 0.0 copy-done.1
  3.1 0.0 copy-start.2
  3.1 1.5 %copy.8.k_ref = bf16[1,256,2240]{2,1,0:T(8,128)(2,1)} copy(bf16[1,256,2240]{1,2,0:T(8,128)(2,1)S(1)} %copy-done.1) | data formatting | bytes 2293760 | tf_op args[1]
  4.6 0.0 copy-done.2
  4.6 0.0 copy-start.3
  4.6 1.5 %copy.9.v_ref = bf16[1,256,2240]{2,1,0:T(8,128)(2,1)} copy(bf16[1,256,2240]{1,2,0:T(8,128)(2,1)S(1)} %copy-done.2) | data formatting | bytes 2293760 | tf_op args[2]
  6.2 0.0 copy-done.3
  6.2 1.5 %copy.10.g_ref = bf16[1,256,2240]{2,1,0:T(8,128)(2,1)} copy(bf16[1,256,2240]{1,2,0:T(8,128)(2,1)S(1)} %copy-done.3) | data formatting | bytes 2293760 | tf_op args[3]
  7.7 119.1 %shard_map.67 = (f32[1,256,2240]{2,1,0:T(8,128)}, f32[1,256,2240]{2,1,0:T(8,128)}, f32[1,256,2240]{2,1,0:T(8,128)}) custom-call(bf16[1,256,2240]{2,1,0:T(8,128)(2,1)} %copy.7.q_ref, bf16[1,256,2240]{2,1,0:T(8,128)(2,1)} %copy.8.k_ref, bf16[1,256,2240]{2,1,0:T(8,128)(2,1)} %copy.9.v_ref, bf16[1,256,2240]{2,1,0:T(8,128)(2,1)} %copy.10.g_ref), custom_call_target="tpu_custom_call" | custom-call | tf_op jit(solution)/shard_map/pallas_call | solution.py:238
  126.8 3.0 %copy.11 = f32[1,256,2240]{1,2,0:T(8,128)} copy(f32[1,256,2240]{2,1,0:T(8,128)} %get-tuple-element.3) | data formatting | bytes 4587520 | tf_op jit(solution)/shard_map/pallas_call | solution.py:238
  129.9 0.0 copy-start
  129.9 3.2 %copy.12 = f32[1,256,2240]{1,2,0:T(8,128)} copy(f32[1,256,2240]{2,1,0:T(8,128)} %get-tuple-element.4) | data formatting | bytes 4587520 | tf_op jit(solution)/shard_map/pallas_call | solution.py:238
  133.0 0.0 copy-done
  133.0 1.9 %copy.13 = f32[1,256,2240]{1,2,0:T(8,128)} copy(f32[1,256,2240]{2,1,0:T(8,128)S(1)} %copy-done) | data formatting | bytes 4587520 | tf_op jit(solution)/shard_map/pallas_call | solution.py:238
Async XLA Ops:
  0.6 2.5 %copy-start.1 = (bf16[1,256,2240]{1,2,0:T(8,128)(2,1)S(1)}, bf16[1,256,2240]{1,2,0:T(8,128)(2,1)}, u32[]{:S(2)}) copy-start(bf16[1,256,2240]{1,2,0:T(8,128)(2,1)} %param.5) | copy-start | bytes 3440644
  3.1 1.5 %copy-start.2 = (bf16[1,256,2240]{1,2,0:T(8,128)(2,1)S(1)}, bf16[1,256,2240]{1,2,0:T(8,128)(2,1)}, u32[]{:S(2)}) copy-start(bf16[1,256,2240]{1,2,0:T(8,128)(2,1)} %param.6) | copy-start | bytes 3440644
  4.6 1.5 %copy-start.3 = (bf16[1,256,2240]{1,2,0:T(8,128)(2,1)S(1)}, bf16[1,256,2240]{1,2,0:T(8,128)(2,1)}, u32[]{:S(2)}) copy-start(bf16[1,256,2240]{1,2,0:T(8,128)(2,1)} %param.7) | copy-start | bytes 3440644
  129.9 3.2 %copy-start = (f32[1,256,2240]{2,1,0:T(8,128)S(1)}, f32[1,256,2240]{2,1,0:T(8,128)}, u32[]{:S(2)}) copy-start(f32[1,256,2240]{2,1,0:T(8,128)} %get-tuple-element.5) | copy-start | bytes 6881284

commit v2 on v1

v2 whole, which is shorter than its diff:
```python
import functools

import jax
import jax.numpy as jnp
from jax import lax
from jax.experimental import pallas as pl
from jax.experimental.pallas import tpu as pltpu
from jax.sharding import PartitionSpec as P

HEADS = 20
HEAD_DIM = 112
LANES = 128
LAG = 2
MESH = pl.DeviceIdType.MESH
NT = (((1,), (1,)), ((), ()))
TN = (((0,), (0,)), ((), ()))


def dot(a, b, dims=(((1,), (0,)), ((), ()))):
    return lax.dot_general(a, b, dims, preferred_element_type=jnp.float32)


def split(state):
    high = state.astype(jnp.bfloat16)
    return high, (state - high.astype(jnp.float32)).astype(jnp.bfloat16)


def kernel(
    n_frame, n_space,
    q_in, k_in, v_in, g_in,
    oq_out, ok_out, ov_out,
    qs, ks, vs, gs, sq, sk, sv,
    local, prefix, total, arrived, send_sem, recv_sem, in_sem, out_sem,
):
    frame, space = lax.axis_index("frame"), lax.axis_index("space")
    levels = max(n_frame - 1, 0).bit_length()
    right_link, left_link = levels, levels + 1

    def place(phase):
        return frame if phase == 0 else n_frame - 1 - frame

    def partner(phase, level):
        at = place(phase)
        other = at ^ (1 << level)
        upper = lax.rem(at // (1 << level), 2) == 1
        exists = other < n_frame
        sends, receives = exists, exists
        if level == levels - 1:
            sends = jnp.logical_and(exists, jnp.logical_not(upper))
            receives = jnp.logical_and(exists, upper)
        return other if phase == 0 else n_frame - 1 - other, upper, exists, sends, receives

    def link(phase, number, h, source):
        if number == right_link:
            device = (frame, space + 1)
        elif number == left_link:
            device = (frame, space - 1)
        else:
            device = (partner(phase, number)[0], space)
        return pltpu.make_async_remote_copy(
            src_ref=source,
            dst_ref=arrived.at[phase, number, h],
            send_sem=send_sem.at[phase, number, h],
            recv_sem=recv_sem.at[phase, number, h],
            device_id=device,
            device_id_type=MESH,
        )

    barrier = pltpu.get_barrier_semaphore()
    greet = [(space + 1 < n_space, (frame, space + 1)), (space > 0, (frame, space - 1))]
    for phase in (0,) if n_frame & (n_frame - 1) == 0 else (0, 1):
        for level in range(levels):
            other, _, exists, _, _ = partner(phase, level)
            greet.append((exists, (other, space)))
    for exists, device in greet:
        @pl.when(exists)
        def _(device=device):
            pl.semaphore_signal(barrier, inc=1, device_id=device, device_id_type=MESH)

    loads = [
        pltpu.make_async_copy(source, target, in_sem.at[i])
        for i, (source, target) in enumerate(((k_in, ks), (v_in, vs), (q_in, qs), (g_in, gs)))
    ]
    for load in loads:
        load.start()

    def begin(phase, h, value):
        local[phase, h] = value
        if phase == 0:
            begin_chain(phase, h)
        else:
            begin_scan(phase, h)

    def begin_scan(phase, h):
        own = (total if phase == 0 else local).at[phase, h]
        prefix[phase, h] = own[...]
        if levels:
            @pl.when(partner(phase, 0)[3])
            def _():
                link(phase, 0, h, own).start()
        elif phase == 1:
            begin_chain(phase, h)

    def scan_source(phase, level, h):
        if level == 0:
            return (total if phase == 0 else local).at[phase, h]
        return arrived.at[phase, level - 1, h]

    def scan_level(phase, level, h):
        _, upper, exists, sends, receives = partner(phase, level)
        source = scan_source(phase, level, h)

        @pl.when(receives)
        def _():
            link(phase, level, h, source).wait_recv()
            came = arrived[phase, level, h]

            @pl.when(upper)
            def _():
                prefix[phase, h] = prefix[phase, h] + came

            if level + 1 < levels:
                arrived[phase, level, h] = came + source[...]

        if level + 1 < levels:
            @pl.when(partner(phase, level + 1)[3])
            def _():
                link(phase, level + 1, h, arrived.at[phase, level, h]).start()
        elif phase == 1:
            begin_chain(phase, h)

    def begin_chain(phase, h):
        own = (local if phase == 0 else prefix).at[phase, h]
        total[phase, h] = own[...]
        if n_space > 1:
            @pl.when(space == 0)
            def _():
                link(phase, right_link, h, own).start()

            @pl.when(space == n_space - 1)
            def _():
                link(phase, left_link, h, own).start()
        elif phase == 0:
            begin_scan(phase, h)

    def chain_hop(phase, hop, h):
        own = (local if phase == 0 else prefix).at[phase, h]
        for number, at in ((right_link, space), (left_link, n_space - 1 - space)):
            @pl.when(at == hop)
            def _(number=number):
                slot = arrived.at[phase, number, h]
                link(phase, number, h, slot).wait_recv()
                came = slot[...]
                total[phase, h] = total[phase, h] + came
                if hop < n_space - 1:
                    slot[...] = came + own[...]
                    link(phase, number, h, slot).start()
        if hop == n_space - 1 and phase == 0:
            begin_scan(phase, h)

    tokens = k_in.shape[2]
    rest = LANES - HEAD_DIM
    row = lax.broadcasted_iota(jnp.int32, (rest, tokens), 0)
    ones = jnp.where(row < 2, 1.0, 0.0).astype(jnp.bfloat16)

    def values(h):
        return jnp.concatenate([vs[h], ones], axis=0)

    def states(h):
        begin(0, h, dot(jnp.maximum(ks[h], 0), values(h), NT))

    def queries(h):
        q = jnp.maximum(qs[h], 0)
        high, low = split(prefix[0, h])
        numerator = dot(jnp.concatenate([high, low], axis=0), jnp.concatenate([q, q], axis=0), TN)
        denominator = numerator[HEAD_DIM:HEAD_DIM + 1] + 1.0
        grad = gs[h].astype(jnp.float32)
        slope = -jnp.sum(grad * numerator[:HEAD_DIM], axis=0, keepdims=True) / (denominator * denominator)
        coarse = slope.astype(jnp.bfloat16).astype(jnp.float32)
        slopes = jnp.where(row == 0, coarse, jnp.where(row == 1, slope - coarse, 0.0))
        scaled = jnp.concatenate([grad / denominator, slopes], axis=0).astype(jnp.bfloat16)
        begin(1, h, dot(q, scaled, NT))
        back = dot(jnp.concatenate([high, low], axis=1), jnp.concatenate([scaled, scaled], axis=0))
        sq[h] = jnp.where(q.astype(jnp.float32) > 0, back, 0.0)
        store(0, h).start()

    def keys(h):
        k = jnp.maximum(ks[h], 0)
        high, low = split(total[1, h])
        wide = dot(jnp.concatenate([high, low], axis=0), jnp.concatenate([k, k], axis=0), TN)
        sv[h] = wide[:HEAD_DIM]
        store(2, h).start()
        value = values(h)
        back = dot(jnp.concatenate([high, low], axis=1), jnp.concatenate([value, value], axis=0))
        sk[h] = jnp.where(k.astype(jnp.float32) > 0, back, 0.0)
        store(1, h).start()

    def store(i, h):
        source, target = ((sq, oq_out), (sk, ok_out), (sv, ov_out))[i]
        return pltpu.make_async_copy(source.at[h], target.at[h], out_sem.at[i, h])

    plan, at = [], 0
    for phase in (0, 1):
        scan = [(functools.partial(scan_level, phase, level), 1 if level == 0 else LAG) for level in range(levels)]
        chain = [(functools.partial(chain_hop, phase, hop), LAG) for hop in range(1, n_space)]
        for act, lag in chain + scan if phase == 0 else scan + chain:
            at += lag
            plan.append((at, act))
        if phase == 0:
            middle = at

    def stage(t, lag, act):
        h = t - lag

        @pl.when(jnp.logical_and(h >= 0, h < HEADS))
        def _():
            act(h)

    def step(t, carry):
        for lag, act in reversed(plan):
            stage(t, lag, act)
        stage(t, 0, states)

        @pl.when(t == middle)
        def _():
            loads[2].wait()
            loads[3].wait()

        stage(t, middle, queries)
        stage(t, at, keys)
        return carry

    loads[0].wait()
    loads[1].wait()
    pl.semaphore_wait(barrier, sum(jnp.int32(exists) for exists, _ in greet))
    lax.fori_loop(0, HEADS + at, step, 0)

    def drain(h, carry):
        for phase in (0, 1):
            for level in range(levels):
                source = scan_source(phase, level, h)

                @pl.when(partner(phase, level)[3])
                def _(source=source, level=level):
                    link(phase, level, h, source).wait_send()
            for number, sends in ((right_link, space < n_space - 1), (left_link, space > 0)):
                @pl.when(sends)
                def _(number=number):
                    link(phase, number, h, prefix.at[phase, h]).wait_send()
        for i in range(3):
            store(i, h).wait()
        return carry

    lax.fori_loop(0, HEADS, drain, 0)


def on_device(n_frame, n_space, *arrays):
    rows = arrays[0].shape[1]
    levels = max(n_frame - 1, 0).bit_length()
    heads = [jnp.swapaxes(array[0], 0, 1).reshape(HEADS, HEAD_DIM, rows) for array in arrays]
    shape = heads[0].shape
    out = jax.ShapeDtypeStruct(shape, jnp.float32)
    state = (HEADS, HEAD_DIM, LANES)
    links = (2, levels + 2, HEADS)
    grads = pl.pallas_call(
        functools.partial(kernel, n_frame, n_space),
        out_shape=(out,) * 3,
        in_specs=[pl.BlockSpec(memory_space=pl.ANY)] * 4,
        out_specs=(pl.BlockSpec(memory_space=pl.ANY),) * 3,
        scratch_shapes=[pltpu.VMEM(shape, jnp.bfloat16)] * 4 + [pltpu.VMEM(shape, jnp.float32)] * 3
        + [pltpu.VMEM((2,) + state, jnp.float32)] * 3
        + [
            pltpu.VMEM((2, levels + 2) + state, jnp.float32),
            pltpu.SemaphoreType.DMA(links),
            pltpu.SemaphoreType.DMA(links),
            pltpu.SemaphoreType.DMA((4,)),
            pltpu.SemaphoreType.DMA((3, HEADS)),
        ],
        compiler_params=pltpu.CompilerParams(
            collective_id=0, has_side_effects=True, vmem_limit_bytes=56 * 1024 * 1024
        ),
    )(*heads)
    return tuple(jnp.swapaxes(grad.reshape(HEADS * HEAD_DIM, rows), 0, 1)[None] for grad in grads)


def solution(mesh):
    placed = P("frame", "space", None)
    return jax.shard_map(
        functools.partial(on_device, mesh.shape["frame"], mesh.shape["space"]),
        mesh=mesh,
        in_specs=(placed,) * 4,
        out_specs=(placed,) * 3,
        check_vma=False,
    )
```

time: 135 us -> 99.9 us (0.74)
  Pallas kernels: 119 us -> 91.9 us
  local copies, waits for them, and re-layouts: 15.2 us -> 7.19 us
    pallas_call x1, Pallas kernels: 119 us -> 91.9 us  [on_device(): pl.pallas_call(functools.partial(kernel, n_frame, n_space), out_shape=(ou...]
    pallas_call x3 -> x0, local copies, waits for them, and re-layouts: 8.12 us -> none  [on_device(): pl.pallas_call(functools.partial(kernel, n_frame, n_space), out_shape=(ou...]
    unnamed x12 -> x7, local copies, waits for them, and re-layouts: 7.05 us -> 7.19 us
where the time goes in v2:
time: 99.9 us; the launch traced here: 99.8 us
  Pallas kernels  91.9 us (92%)
  local copies, waits for them, and re-layouts  7.19 us (7%)
    pallas_call x1, Pallas kernels, on_device(): pl.pallas_call(functools.partial(kernel, n_frame, n_space), out_shape=(ou...  91.9 us
    unnamed x7, local copies, waits for them, and re-layouts  7.19 us

profile of v2, /device:TPU:0, one launch (start us, length us, event | category | flops | bytes accessed | tf_op | source)
XLA Modules:
  0.0 99.8 jit_solution(10791164282630286923)
XLA Ops:
  0.6 91.9 %shard_map.67 = (f32[20,112,256]{2,1,0:T(8,128)}, f32[20,112,256]{2,1,0:T(8,128)}, f32[20,112,256]{2,1,0:T(8,128)}) custom-call(bf16[20,112,256]{2,1,0:T(8,128)(2,1)} %bitcast.38, bf16[20,112,256]{2,1,0:T(8,128)(2,1)} %bitcast.39, bf16[20,112,256]{2,1,0:T(8,128)(2,1)} %bitcast.40, bf16[20,112,256]{2,1,0:T(8,128)(2,1)} %bitcast.41), custom_call_target="tpu_custom_call" | custom-call | tf_op jit(solution)/shard_map/pallas_call | solution.py:265
  92.6 0.0 copy-start.1
  92.6 3.3 %copy.10 = f32[1,256,2240]{1,2,0:T(8,128)} copy(f32[1,256,2240]{1,2,0:T(8,128)} %bitcast.37) | data formatting | bytes 4587520
  95.9 0.0 copy-done.1
  95.9 0.0 copy-start
  95.9 1.4 %copy.11 = f32[1,256,2240]{1,2,0:T(8,128)} copy(f32[1,256,2240]{1,2,0:T(8,128)S(1)} %bitcast.36) | data formatting | bytes 4587520
  97.3 1.1 %copy-done = f32[20,112,256]{2,1,0:T(8,128)S(1)} copy-done((f32[20,112,256]{2,1,0:T(8,128)S(1)}, f32[20,112,256]{2,1,0:T(8,128)}, u32[]{:S(2)}) %copy-start) | copy-done | bytes 2293784
  98.4 1.4 %copy.12 = f32[1,256,2240]{1,2,0:T(8,128)} copy(f32[1,256,2240]{1,2,0:T(8,128)S(1)} %bitcast.35) | data formatting | bytes 4587520
Async XLA Ops:
  92.6 3.3 %copy-start.1 = (f32[20,112,256]{2,1,0:T(8,128)S(1)}, f32[20,112,256]{2,1,0:T(8,128)}, u32[]{:S(2)}) copy-start(f32[20,112,256]{2,1,0:T(8,128)} %get-tuple-element.7) | copy-start | bytes 6881284
  95.9 2.5 %copy-start = (f32[20,112,256]{2,1,0:T(8,128)S(1)}, f32[20,112,256]{2,1,0:T(8,128)}, u32[]{:S(2)}) copy-start(f32[20,112,256]{2,1,0:T(8,128)} %get-tuple-element.8) | copy-start | bytes 6881284

commit v3 on v2

v3 whole, which is shorter than its diff:
```python
import functools

import jax
import jax.numpy as jnp
from jax import lax
from jax.experimental import pallas as pl
from jax.experimental.pallas import tpu as pltpu
from jax.sharding import PartitionSpec as P

HEADS = 20
HEAD_DIM = 112
LANES = 128
LAG = 2
MESH = pl.DeviceIdType.MESH
NT = (((1,), (1,)), ((), ()))
TN = (((0,), (0,)), ((), ()))


def dot(a, b, dims=(((1,), (0,)), ((), ()))):
    return lax.dot_general(a, b, dims, preferred_element_type=jnp.float32)


def split(state):
    high = state.astype(jnp.bfloat16)
    return high, (state - high.astype(jnp.float32)).astype(jnp.bfloat16)


def guard(condition, act):
    if condition is True:
        act()
    else:
        pl.when(condition)(act)


def both(*conditions):
    left = [condition for condition in conditions if condition is not True]
    return functools.reduce(jnp.logical_and, left) if left else True


def ones_below(tokens):
    row = lax.broadcasted_iota(jnp.int32, (LANES - HEAD_DIM, tokens), 0)
    return row, jnp.where(row < 2, 1.0, 0.0).astype(jnp.bfloat16)


def kernel(
    n_frame, n_space,
    q_in, k_in, v_in, g_in,
    state_out, grad_out, scaled_out,
    qs, ks, vs, gs, scaleds,
    local, prefix, total, arrived, send_sem, recv_sem, in_sem, out_sem,
):
    frame, space = lax.axis_index("frame"), lax.axis_index("space")
    levels = max(n_frame - 1, 0).bit_length()
    right_link, left_link = levels, levels + 1

    def place(phase):
        return frame if phase == 0 else n_frame - 1 - frame

    def partner(phase, level):
        at = place(phase)
        other = at ^ (1 << level)
        upper = lax.rem(at // (1 << level), 2) == 1
        exists = True if n_frame & (n_frame - 1) == 0 else other < n_frame
        sends, receives = exists, exists
        if level == levels - 1:
            sends, receives = both(exists, jnp.logical_not(upper)), both(exists, upper)
        return other if phase == 0 else n_frame - 1 - other, upper, exists, sends, receives

    def link(phase, number, h, source):
        if number == right_link:
            device = (frame, space + 1)
        elif number == left_link:
            device = (frame, space - 1)
        else:
            device = (partner(phase, number)[0], space)
        return pltpu.make_async_remote_copy(
            src_ref=source,
            dst_ref=arrived.at[phase, number, h],
            send_sem=send_sem.at[phase, number, h],
            recv_sem=recv_sem.at[phase, number, h],
            device_id=device,
            device_id_type=MESH,
        )

    barrier = pltpu.get_barrier_semaphore()
    greet = [(space + 1 < n_space, (frame, space + 1)), (space > 0, (frame, space - 1))]
    for phase in (0,) if n_frame & (n_frame - 1) == 0 else (0, 1):
        for level in range(levels):
            other, _, exists, _, _ = partner(phase, level)
            greet.append((exists, (other, space)))
    for exists, device in greet:
        guard(exists, functools.partial(
            pl.semaphore_signal, barrier, inc=1, device_id=device, device_id_type=MESH))

    loads = [
        pltpu.make_async_copy(source, target, in_sem.at[i])
        for i, (source, target) in enumerate(((k_in, ks), (v_in, vs), (q_in, qs), (g_in, gs)))
    ]
    for load in loads:
        load.start()

    def begin(phase, h, value):
        local[phase, h] = value
        if phase == 0:
            begin_chain(phase, h)
        else:
            begin_scan(phase, h)

    def begin_scan(phase, h):
        own = scan_source(phase, 0, h)
        prefix[phase, h] = own[...]
        if levels:
            guard(partner(phase, 0)[3], lambda: link(phase, 0, h, own).start())
        elif phase == 1:
            begin_chain(phase, h)

    def scan_source(phase, level, h):
        if level == 0:
            return (total if phase == 0 else local).at[phase, h]
        return arrived.at[phase, level - 1, h]

    def scan_level(phase, level, h):
        _, upper, exists, sends, receives = partner(phase, level)
        source = scan_source(phase, level, h)

        def take():
            link(phase, level, h, source).wait_recv()
            came = arrived[phase, level, h]
            if level + 1 < levels:
                prefix[phase, h] = prefix[phase, h] + jnp.where(upper, came, 0.0)
                arrived[phase, level, h] = came + source[...]
            else:
                prefix[phase, h] = prefix[phase, h] + came

        guard(receives, take)
        if level + 1 < levels:
            follow = arrived.at[phase, level, h]
            guard(partner(phase, level + 1)[3], lambda: link(phase, level + 1, h, follow).start())
        elif phase == 1:
            begin_chain(phase, h)

    def chain_own(phase, h):
        return (local if phase == 0 else prefix).at[phase, h]

    def begin_chain(phase, h):
        own = chain_own(phase, h)
        total[phase, h] = own[...]
        if n_space > 1:
            guard(space == 0, lambda: link(phase, right_link, h, own).start())
            guard(space == n_space - 1, lambda: link(phase, left_link, h, own).start())

    def chain_hop(phase, number, at, h):
        slot = arrived.at[phase, number, h]
        link(phase, number, h, slot).wait_recv()
        came = slot[...]
        total[phase, h] = total[phase, h] + came

        def forward():
            slot[...] = came + chain_own(phase, h)[...]
            link(phase, number, h, slot).start()

        guard(at < n_space - 1, forward)

    tokens = k_in.shape[2]
    row, ones = ones_below(tokens)

    def values(h):
        return jnp.concatenate([vs[h], ones], axis=0)

    def states(h):
        begin(0, h, dot(jnp.maximum(ks[h], 0), values(h), NT))

    def queries(h):
        q = jnp.maximum(qs[h], 0)
        store(0, h).start()
        pair = jnp.concatenate(split(prefix[0, h]), axis=0)
        numerator = dot(pair, jnp.concatenate([q, q], axis=0), TN)
        inverse = 1.0 / (numerator[HEAD_DIM:HEAD_DIM + 1] + 1.0)
        grad = gs[h].astype(jnp.float32)
        slope = -jnp.sum(grad * numerator[:HEAD_DIM], axis=0, keepdims=True) * inverse * inverse
        coarse = slope.astype(jnp.bfloat16).astype(jnp.float32)
        slopes = jnp.where(row == 0, coarse, jnp.where(row == 1, slope - coarse, 0.0))
        scaled = jnp.concatenate([grad * inverse, slopes], axis=0).astype(jnp.bfloat16)
        begin(1, h, dot(q, scaled, NT))
        scaleds[h] = scaled
        store(2, h).start()

    def keys(h):
        store(1, h).start()

    def store(i, h):
        source, target = ((prefix.at[0], state_out), (total.at[1], grad_out), (scaleds, scaled_out))[i]
        return pltpu.make_async_copy(source.at[h], target.at[h], out_sem.at[i, h])

    plan = []

    def plan_scan(phase, at):
        for level in range(levels):
            at += 1 if level == 0 else LAG
            plan.insert(0, (at, True, functools.partial(scan_level, phase, level)))
        return at

    def plan_chain(phase, at):
        for number, place in ((right_link, space), (left_link, n_space - 1 - space)):
            if n_space > 1:
                plan.insert(0, (at + LAG * place, place > 0, functools.partial(chain_hop, phase, number, place)))
        return at + LAG * (n_space - 1)

    turn = plan_chain(0, 0)
    middle = plan_scan(0, turn)
    last = plan_chain(1, plan_scan(1, middle))

    def stage(t, lag, condition, act):
        h = t - lag
        guard(both(h >= 0, h < HEADS, condition), lambda: act(h))

    def step(t, carry):
        for lag, condition, act in plan:
            stage(t, lag, condition, act)
        stage(t, turn, True, functools.partial(begin_scan, 0))
        stage(t, 0, True, states)

        @pl.when(t == middle)
        def _():
            loads[2].wait()
            loads[3].wait()

        stage(t, middle, True, queries)
        stage(t, last, True, keys)
        return carry

    loads[0].wait()
    loads[1].wait()
    pl.semaphore_wait(barrier, sum(jnp.int32(exists) for exists, _ in greet))
    lax.fori_loop(0, HEADS + last, step, 0)

    def drain(h, carry):
        for phase in (0, 1):
            for level in range(levels):
                guard(partner(phase, level)[3], link(phase, level, h, scan_source(phase, level, h)).wait_send)
            own = chain_own(phase, h)
            if n_space > 1:
                guard(space < n_space - 1, link(phase, right_link, h, own).wait_send)
                guard(space > 0, link(phase, left_link, h, own).wait_send)
        for i in range(3):
            store(i, h).wait()
        return carry

    lax.fori_loop(0, HEADS, drain, 0)


def products(state, grad, scaled, q, k, v, query_grad, key_grad, value_grad):
    _, ones = ones_below(k.shape[2])
    for h in range(q.shape[0]):
        wide = jnp.concatenate(split(state[h]), axis=1)
        back = dot(wide, jnp.concatenate([scaled[h], scaled[h]], axis=0))
        query_grad[h] = jnp.where(q[h].astype(jnp.float32) > 0, back, 0.0)
        high, low = split(grad[h])
        feature = jnp.maximum(k[h], 0)
        value_grad[h] = dot(
            jnp.concatenate([high[:, :HEAD_DIM], low[:, :HEAD_DIM]], axis=0),
            jnp.concatenate([feature, feature], axis=0), TN)
        value = jnp.concatenate([v[h], ones], axis=0)
        back = dot(jnp.concatenate([high, low], axis=1), jnp.concatenate([value, value], axis=0))
        key_grad[h] = jnp.where(k[h].astype(jnp.float32) > 0, back, 0.0)


def on_device(n_frame, n_space, *arrays):
    rows = arrays[0].shape[1]
    levels = max(n_frame - 1, 0).bit_length()
    heads = [jnp.swapaxes(array[0], 0, 1).reshape(HEADS, HEAD_DIM, rows) for array in arrays]
    shape = heads[0].shape
    state = (HEADS, HEAD_DIM, LANES)
    wide = (HEADS, LANES, rows)
    links = (2, levels + 2, HEADS)
    states = pl.pallas_call(
        functools.partial(kernel, n_frame, n_space),
        out_shape=(
            jax.ShapeDtypeStruct(state, jnp.float32),
            jax.ShapeDtypeStruct(state, jnp.float32),
            jax.ShapeDtypeStruct(wide, jnp.bfloat16),
        ),
        in_specs=[pl.BlockSpec(memory_space=pl.ANY)] * 4,
        out_specs=(pl.BlockSpec(memory_space=pl.ANY),) * 3,
        scratch_shapes=[pltpu.VMEM(shape, jnp.bfloat16)] * 4 + [pltpu.VMEM(wide, jnp.bfloat16)]
        + [pltpu.VMEM((2,) + state, jnp.float32)] * 3
        + [
            pltpu.VMEM((2, levels + 2) + state, jnp.float32),
            pltpu.SemaphoreType.DMA(links),
            pltpu.SemaphoreType.DMA(links),
            pltpu.SemaphoreType.DMA((4,)),
            pltpu.SemaphoreType.DMA((3, HEADS)),
        ],
        compiler_params=pltpu.CompilerParams(
            collective_id=0, has_side_effects=True, vmem_limit_bytes=40 * 1024 * 1024
        ),
    )(*heads)
    group = max(n for n in range(1, 6) if HEADS % n == 0)

    def some(whole):
        return pl.BlockSpec((group,) + whole[1:], lambda i: (i, 0, 0))

    grads = pl.pallas_call(
        products,
        grid=(HEADS // group,),
        out_shape=(jax.ShapeDtypeStruct(shape, jnp.float32),) * 3,
        in_specs=[some(state), some(state), some(wide)] + [some(shape)] * 3,
        out_specs=(some(shape),) * 3,
        compiler_params=pltpu.CompilerParams(vmem_limit_bytes=24 * 1024 * 1024),
    )(*states, *heads[:3])
    return tuple(jnp.swapaxes(grad.reshape(HEADS * HEAD_DIM, rows), 0, 1)[None] for grad in grads)


def solution(mesh):
    placed = P("frame", "space", None)
    return jax.shard_map(
        functools.partial(on_device, mesh.shape["frame"], mesh.shape["space"]),
        mesh=mesh,
        in_specs=(placed,) * 4,
        out_specs=(placed,) * 3,
        check_vma=False,
    )
```

time: 99.9 us -> 99.4 us (level)
  local copies, waits for them, and re-layouts: 7.19 us -> 5.03 us
  Pallas kernels: 91.9 us -> 93.4 us
    unnamed x7 -> x8, local copies, waits for them, and re-layouts: 7.19 us -> 5.03 us
    pallas_call x1 -> x2, Pallas kernels: 91.9 us -> 93.4 us  [the longest x1 89.7 us: on_device(): pl.pallas_call(functools.partial(kernel, n_frame, n_space), out_shape=(ja...]
where the time goes in v3:
time: 99.4 us; the launch traced here: 99.1 us
  Pallas kernels  93.4 us (94%)
  local copies, waits for them, and re-layouts  5.03 us (5%)
    pallas_call x1, Pallas kernels, on_device(): pl.pallas_call(functools.partial(kernel, n_frame, n_space), out_shape=(ja...  89.7 us
    unnamed x8, local copies, waits for them, and re-layouts  5.03 us
    pallas_call x1, Pallas kernels, on_device(): pl.pallas_call(products, grid=(HEADS // group,), out_shape=(jax.ShapeDtyp...  3.76 us

profile of v3, /device:TPU:0, one launch (start us, length us, event | category | flops | bytes accessed | tf_op | source)
XLA Modules:
  0.0 99.1 jit_solution(8410469850007968640)
XLA Ops:
  0.6 0.0 copy-start
  0.6 1.2 %copy-done = bf16[1,256,2240]{1,2,0:T(8,128)(2,1)S(1)} copy-done((bf16[1,256,2240]{1,2,0:T(8,128)(2,1)S(1)}, bf16[1,256,2240]{1,2,0:T(8,128)(2,1)}, u32[]{:S(2)}) %copy-start) | copy-done | bytes 1146904
  1.9 0.0 copy-start.1
  1.9 1.3 %copy-done.1 = bf16[1,256,2240]{1,2,0:T(8,128)(2,1)S(1)} copy-done((bf16[1,256,2240]{1,2,0:T(8,128)(2,1)S(1)}, bf16[1,256,2240]{1,2,0:T(8,128)(2,1)}, u32[]{:S(2)}) %copy-start.1) | copy-done | bytes 1146904
  3.2 0.0 copy-start.2
  3.2 1.3 %copy-done.2 = bf16[1,256,2240]{1,2,0:T(8,128)(2,1)S(1)} copy-done((bf16[1,256,2240]{1,2,0:T(8,128)(2,1)S(1)}, bf16[1,256,2240]{1,2,0:T(8,128)(2,1)}, u32[]{:S(2)}) %copy-start.2) | copy-done | bytes 1146904
  4.4 0.0 copy-start.3
  4.4 1.3 %copy-done.3 = bf16[1,256,2240]{1,2,0:T(8,128)(2,1)S(1)} copy-done((bf16[1,256,2240]{1,2,0:T(8,128)(2,1)S(1)}, bf16[1,256,2240]{1,2,0:T(8,128)(2,1)}, u32[]{:S(2)}) %copy-start.3) | copy-done | bytes 1146904
  5.7 89.7 %shard_map.67 = (f32[20,112,128]{2,1,0:T(8,128)S(1)}, f32[20,112,128]{2,1,0:T(8,128)S(1)}, bf16[20,128,256]{2,1,0:T(8,128)(2,1)S(1)}) custom-call(bf16[20,112,256]{2,1,0:T(8,128)(2,1)S(1)} %bitcast.35, bf16[20,112,256]{2,1,0:T(8,128)(2,1)S(1)} %bitcast.37, bf16[20,112,256]{2,1,0:T(8,128)(2,1)S(1)} %bitcast.39, bf16[20,112,256]{2,1,0:T(8,128)(2,1)S(1)} %bitcast.41), custom_call_target="tpu_custom_call" | custom-call | tf_op jit(solution)/shard_map/pallas_call | solution.py:276
  95.4 3.8 %shard_map.68 = (f32[20,112,256]{2,1,0:T(8,128)}, f32[20,112,256]{2,1,0:T(8,128)}, f32[20,112,256]{2,1,0:T(8,128)}) custom-call(f32[20,112,128]{2,1,0:T(8,128)S(1)} %get-tuple-element.9.state, f32[20,112,128]{2,1,0:T(8,128)S(1)} %get-tuple-element.10.grad, bf16[20,128,256]{2,1,0:T(8,128)(2,1)S(1)} %get-tuple-element.11.scaled, ...), custom_call_target="tpu_custom_call" | custom-call | tf_op jit(solution)/shard_map/pallas_call | solution.py:303
Async XLA Ops:
  0.6 1.3 %copy-start = (bf16[1,256,2240]{1,2,0:T(8,128)(2,1)S(1)}, bf16[1,256,2240]{1,2,0:T(8,128)(2,1)}, u32[]{:S(2)}) copy-start(bf16[1,256,2240]{1,2,0:T(8,128)(2,1)} %param.4) | copy-start | bytes 3440644
  1.9 1.3 %copy-start.1 = (bf16[1,256,2240]{1,2,0:T(8,128)(2,1)S(1)}, bf16[1,256,2240]{1,2,0:T(8,128)(2,1)}, u32[]{:S(2)}) copy-start(bf16[1,256,2240]{1,2,0:T(8,128)(2,1)} %param.5) | copy-start | bytes 3440644
  3.2 1.3 %copy-start.2 = (bf16[1,256,2240]{1,2,0:T(8,128)(2,1)S(1)}, bf16[1,256,2240]{1,2,0:T(8,128)(2,1)}, u32[]{:S(2)}) copy-start(bf16[1,256,2240]{1,2,0:T(8,128)(2,1)} %param.6) | copy-start | bytes 3440644
  4.4 1.3 %copy-start.3 = (bf16[1,256,2240]{1,2,0:T(8,128)(2,1)S(1)}, bf16[1,256,2240]{1,2,0:T(8,128)(2,1)}, u32[]{:S(2)}) copy-start(bf16[1,256,2240]{1,2,0:T(8,128)(2,1)} %param.7) | copy-start | bytes 3440644

commit v4 on v3

--- a/solution.py
+++ b/solution.py
@@ -11,6 +11,7 @@
 HEAD_DIM = 112
 LANES = 128
 LAG = 2
+GROUP = 5
 MESH = pl.DeviceIdType.MESH
 NT = (((1,), (1,)), ((), ()))
 TN = (((0,), (0,)), ((), ()))
@@ -92,12 +93,21 @@
         guard(exists, functools.partial(
             pl.semaphore_signal, barrier, inc=1, device_id=device, device_id_type=MESH))
 
-    loads = [
-        pltpu.make_async_copy(source, target, in_sem.at[i])
-        for i, (source, target) in enumerate(((k_in, ks), (v_in, vs), (q_in, qs), (g_in, gs)))
-    ]
-    for load in loads:
-        load.start()
+    def load(i, part):
+        source, target = ((k_in, ks), (v_in, vs), (q_in, qs), (g_in, gs))[i]
+        some = pl.ds(part * GROUP, GROUP)
+        return pltpu.make_async_copy(source.at[some], target.at[some], in_sem.at[i, part])
+
+    for pair in ((0, 1), (2, 3)):
+        for part in range(HEADS // GROUP):
+            for i in pair:
+                load(i, part).start()
+
+    def loaded(pair, h):
+        @pl.when(lax.rem(h, GROUP) == 0)
+        def _():
+            for i in pair:
+                load(i, h // GROUP).wait()
 
     def begin(phase, h, value):
         local[phase, h] = value
@@ -168,9 +178,11 @@
         return jnp.concatenate([vs[h], ones], axis=0)
 
     def states(h):
+        loaded((0, 1), h)
         begin(0, h, dot(jnp.maximum(ks[h], 0), values(h), NT))
 
     def queries(h):
+        loaded((2, 3), h)
         q = jnp.maximum(qs[h], 0)
         store(0, h).start()
         pair = jnp.concatenate(split(prefix[0, h]), axis=0)
@@ -196,7 +208,7 @@
 
     def plan_scan(phase, at):
         for level in range(levels):
-            at += 1 if level == 0 else LAG
+            at += LAG
             plan.insert(0, (at, True, functools.partial(scan_level, phase, level)))
         return at
 
@@ -219,18 +231,10 @@
             stage(t, lag, condition, act)
         stage(t, turn, True, functools.partial(begin_scan, 0))
         stage(t, 0, True, states)
-
-        @pl.when(t == middle)
-        def _():
-            loads[2].wait()
-            loads[3].wait()
-
         stage(t, middle, True, queries)
         stage(t, last, True, keys)
         return carry
 
-    loads[0].wait()
-    loads[1].wait()
     pl.semaphore_wait(barrier, sum(jnp.int32(exists) for exists, _ in greet))
     lax.fori_loop(0, HEADS + last, step, 0)
 
@@ -280,7 +284,7 @@
             jax.ShapeDtypeStruct(state, jnp.float32),
             jax.ShapeDtypeStruct(wide, jnp.bfloat16),
         ),
-        in_specs=[pl.BlockSpec(memory_space=pl.ANY)] * 4,
+        in_specs=[pl.BlockSpec(memory_space=pltpu.HBM)] * 4,
         out_specs=(pl.BlockSpec(memory_space=pl.ANY),) * 3,
         scratch_shapes=[pltpu.VMEM(shape, jnp.bfloat16)] * 4 + [pltpu.VMEM(wide, jnp.bfloat16)]
         + [pltpu.VMEM((2,) + state, jnp.float32)] * 3
@@ -288,21 +292,19 @@
             pltpu.VMEM((2, levels + 2) + state, jnp.float32),
             pltpu.SemaphoreType.DMA(links),
             pltpu.SemaphoreType.DMA(links),
-            pltpu.SemaphoreType.DMA((4,)),
+            pltpu.SemaphoreType.DMA((4, HEADS // GROUP)),
             pltpu.SemaphoreType.DMA((3, HEADS)),
         ],
         compiler_params=pltpu.CompilerParams(
-            collective_id=0, has_side_effects=True, vmem_limit_bytes=40 * 1024 * 1024
+            collective_id=0, has_side_effects=True, vmem_limit_bytes=56 * 1024 * 1024
         ),
     )(*heads)
-    group = max(n for n in range(1, 6) if HEADS % n == 0)
-
     def some(whole):
-        return pl.BlockSpec((group,) + whole[1:], lambda i: (i, 0, 0))
+        return pl.BlockSpec((GROUP,) + whole[1:], lambda i: (i, 0, 0))
 
     grads = pl.pallas_call(
         products,
-        grid=(HEADS // group,),
+        grid=(HEADS // GROUP,),
         out_shape=(jax.ShapeDtypeStruct(shape, jnp.float32),) * 3,
         in_specs=[some(state), some(state), some(wide)] + [some(shape)] * 3,
         out_specs=(some(shape),) * 3,

time: 99.4 us -> 101 us (1.016)
  Pallas kernels: 93.4 us -> 96 us
  local copies, waits for them, and re-layouts: 5.03 us -> 3.84 us
    pallas_call x1, Pallas kernels: 89.7 us -> 92.3 us  [on_device(): pl.pallas_call(functools.partial(kernel, n_frame, n_space), out_shape=(ja...]
    unnamed x8 -> x12, local copies, waits for them, and re-layouts: 5.03 us -> 3.84 us
where the time goes in v4:
time: 101 us
  Pallas kernels  96 us (95%)
  local copies, waits for them, and re-layouts  3.84 us (4%)
    pallas_call x1, Pallas kernels, on_device(): pl.pallas_call(functools.partial(kernel, n_frame, n_space), out_shape=(ja...  92.3 us
    unnamed x12, local copies, waits for them, and re-layouts  3.84 us
    pallas_call x1, Pallas kernels, on_device(): pl.pallas_call(products, grid=(HEADS // GROUP,), out_shape=(jax.ShapeDtyp...  3.73 us

profile of v4, /device:TPU:0, one launch (start us, length us, event | category | flops | bytes accessed | tf_op | source)
XLA Modules:
  0.0 100.5 jit_solution(9533158245258102913)
XLA Ops:
  0.6 0.0 copy-start
  0.6 0.0 copy-start.1
  0.7 0.0 copy-start.2
  0.7 92.3 %shard_map.67 = (f32[20,112,128]{2,1,0:T(8,128)}, f32[20,112,128]{2,1,0:T(8,128)}, bf16[20,128,256]{2,1,0:T(8,128)(2,1)}) custom-call(bf16[20,112,256]{2,1,0:T(8,128)(2,1)} %bitcast.35, bf16[20,112,256]{2,1,0:T(8,128)(2,1)} %bitcast.37, bf16[20,112,256]{2,1,0:T(8,128)(2,1)} %bitcast.39, bf16[20,112,256]{2,1,0:T(8,128)(2,1)} %bitcast.41), custom_call_target="tpu_custom_call" | custom-call | tf_op jit(solution)/shard_map/pallas_call | solution.py:280
  92.9 0.0 copy-done
  93.0 0.0 copy-done.1
  93.0 0.0 copy-done.2
  93.0 0.0 copy-start.3
  93.0 1.3 %copy-done.3 = bf16[20,128,256]{2,1,0:T(8,128)(2,1)S(1)} copy-done((bf16[20,128,256]{2,1,0:T(8,128)(2,1)S(1)}, bf16[20,128,256]{2,1,0:T(8,128)(2,1)}, u32[]{:S(2)}) %copy-start.3) | copy-done | bytes 1310744
  94.3 0.0 copy-start.4
  94.3 1.3 %copy-done.4 = f32[20,112,128]{2,1,0:T(8,128)S(1)} copy-done((f32[20,112,128]{2,1,0:T(8,128)S(1)}, f32[20,112,128]{2,1,0:T(8,128)}, u32[]{:S(2)}) %copy-start.4) | copy-done | bytes 1146904
  95.6 0.0 copy-start.5
  95.6 1.3 %copy-done.5 = f32[20,112,128]{2,1,0:T(8,128)S(1)} copy-done((f32[20,112,128]{2,1,0:T(8,128)S(1)}, f32[20,112,128]{2,1,0:T(8,128)}, u32[]{:S(2)}) %copy-start.5) | copy-done | bytes 1146904
  96.8 3.7 %shard_map.68 = (f32[20,112,256]{2,1,0:T(8,128)}, f32[20,112,256]{2,1,0:T(8,128)}, f32[20,112,256]{2,1,0:T(8,128)}) custom-call(f32[20,112,128]{2,1,0:T(8,128)S(1)} %copy-done.4, f32[20,112,128]{2,1,0:T(8,128)S(1)} %copy-done.5, bf16[20,128,256]{2,1,0:T(8,128)(2,1)S(1)} %copy-done.3, bf16[20,112,256]{2,1,0:T(8,128)(2,1)S(1)} %bitcast.36, ...), custom_call_target="tpu_custom_call" | custom-call | tf_op jit(solution)/shard_map/pallas_call | solution.py:305
Async XLA Ops:
  0.6 92.3 %copy-start = (bf16[1,256,2240]{1,2,0:T(8,128)(2,1)S(1)}, bf16[1,256,2240]{1,2,0:T(8,128)(2,1)}, u32[]{:S(2)}) copy-start(bf16[1,256,2240]{1,2,0:T(8,128)(2,1)} %param.4) | copy-start | bytes 3440644
  0.6 92.3 %copy-start.1 = (bf16[1,256,2240]{1,2,0:T(8,128)(2,1)S(1)}, bf16[1,256,2240]{1,2,0:T(8,128)(2,1)}, u32[]{:S(2)}) copy-start(bf16[1,256,2240]{1,2,0:T(8,128)(2,1)} %param.5) | copy-start | bytes 3440644
  0.7 92.3 %copy-start.2 = (bf16[1,256,2240]{1,2,0:T(8,128)(2,1)S(1)}, bf16[1,256,2240]{1,2,0:T(8,128)(2,1)}, u32[]{:S(2)}) copy-start(bf16[1,256,2240]{1,2,0:T(8,128)(2,1)} %param.6) | copy-start | bytes 3440644
  93.0 1.3 %copy-start.3 = (bf16[20,128,256]{2,1,0:T(8,128)(2,1)S(1)}, bf16[20,128,256]{2,1,0:T(8,128)(2,1)}, u32[]{:S(2)}) copy-start(bf16[20,128,256]{2,1,0:T(8,128)(2,1)} %get-tuple-element.11.scaled) | copy-start | bytes 3932164
  94.3 1.3 %copy-start.4 = (f32[20,112,128]{2,1,0:T(8,128)S(1)}, f32[20,112,128]{2,1,0:T(8,128)}, u32[]{:S(2)}) copy-start(f32[20,112,128]{2,1,0:T(8,128)} %get-tuple-element.9.state) | copy-start | bytes 3440644
  95.6 1.3 %copy-start.5 = (f32[20,112,128]{2,1,0:T(8,128)S(1)}, f32[20,112,128]{2,1,0:T(8,128)}, u32[]{:S(2)}) copy-start(f32[20,112,128]{2,1,0:T(8,128)} %get-tuple-element.10.grad) | copy-start | bytes 3440644

commit v5 on v4

--- a/solution.py
+++ b/solution.py
@@ -48,7 +48,7 @@
     q_in, k_in, v_in, g_in,
     state_out, grad_out, scaled_out,
     qs, ks, vs, gs, scaleds,
-    local, prefix, total, arrived, send_sem, recv_sem, in_sem, out_sem,
+    local, prefix, total, arrived, send_sem, recv_sem, share_send, share_recv, in_sem, out_sem,
 ):
     frame, space = lax.axis_index("frame"), lax.axis_index("space")
     levels = max(n_frame - 1, 0).bit_length()
@@ -67,6 +67,24 @@
             sends, receives = both(exists, jnp.logical_not(upper)), both(exists, upper)
         return other if phase == 0 else n_frame - 1 - other, upper, exists, sends, receives
 
+    def halves(level):
+        return 0 < level < levels and n_frame % 2 == 0
+
+    def half(phase):
+        rows = HEAD_DIM // 2
+        return pl.ds(pl.multiple_of(lax.rem(place(phase), 2) * rows, 8), rows)
+
+    def share(phase, level, h):
+        part = arrived.at[phase, level, h, half(phase)]
+        return pltpu.make_async_remote_copy(
+            src_ref=part,
+            dst_ref=part,
+            send_sem=share_send.at[phase, level, h],
+            recv_sem=share_recv.at[phase, level, h],
+            device_id=(partner(phase, 0)[0], space),
+            device_id_type=MESH,
+        )
+
     def link(phase, number, h, source):
         if number == right_link:
             device = (frame, space + 1)
@@ -74,9 +92,12 @@
             device = (frame, space - 1)
         else:
             device = (partner(phase, number)[0], space)
+        target = arrived.at[phase, number, h]
+        if halves(number):
+            source, target = source.at[half(phase)], target.at[half(phase)]
         return pltpu.make_async_remote_copy(
             src_ref=source,
-            dst_ref=arrived.at[phase, number, h],
+            dst_ref=target,
             send_sem=send_sem.at[phase, number, h],
             recv_sem=recv_sem.at[phase, number, h],
             device_id=device,
@@ -129,12 +150,22 @@
             return (total if phase == 0 else local).at[phase, h]
         return arrived.at[phase, level - 1, h]
 
+    def pass_on(phase, level, h):
+        def act():
+            link(phase, level, h, scan_source(phase, level, h)).wait_recv()
+            share(phase, level, h).start()
+
+        guard(partner(phase, level)[4], act)
+
     def scan_level(phase, level, h):
         _, upper, exists, sends, receives = partner(phase, level)
         source = scan_source(phase, level, h)
 
         def take():
-            link(phase, level, h, source).wait_recv()
+            if halves(level):
+                share(phase, level, h).wait()
+            else:
+                link(phase, level, h, source).wait_recv()
             came = arrived[phase, level, h]
             if level + 1 < levels:
                 prefix[phase, h] = prefix[phase, h] + jnp.where(upper, came, 0.0)
@@ -209,6 +240,9 @@
     def plan_scan(phase, at):
         for level in range(levels):
             at += LAG
+            if halves(level):
+                plan.insert(0, (at, True, functools.partial(pass_on, phase, level)))
+                at += 1
             plan.insert(0, (at, True, functools.partial(scan_level, phase, level)))
         return at
 
@@ -292,6 +326,8 @@
             pltpu.VMEM((2, levels + 2) + state, jnp.float32),
             pltpu.SemaphoreType.DMA(links),
             pltpu.SemaphoreType.DMA(links),
+            pltpu.SemaphoreType.DMA(links),
+            pltpu.SemaphoreType.DMA(links),
             pltpu.SemaphoreType.DMA((4, HEADS // GROUP)),
             pltpu.SemaphoreType.DMA((3, HEADS)),
         ],
@@ -308,7 +344,7 @@
         out_shape=(jax.ShapeDtypeStruct(shape, jnp.float32),) * 3,
         in_specs=[some(state), some(state), some(wide)] + [some(shape)] * 3,
         out_specs=(some(shape),) * 3,
-        compiler_params=pltpu.CompilerParams(vmem_limit_bytes=24 * 1024 * 1024),
+        compiler_params=pltpu.CompilerParams(vmem_limit_bytes=56 * 1024 * 1024),
     )(*states, *heads[:3])
     return tuple(jnp.swapaxes(grad.reshape(HEADS * HEAD_DIM, rows), 0, 1)[None] for grad in grads)
 

time: 101 us -> 99.2 us (0.982)
  local copies, waits for them, and re-layouts: 3.84 us -> 0 us
  Pallas kernels: 96 us -> 98.4 us
    unnamed x12 -> x0, local copies, waits for them, and re-layouts: 3.84 us -> none
    pallas_call x1, Pallas kernels: 3.73 us -> 6.67 us  [on_device(): pl.pallas_call(products, grid=(HEADS // GROUP,), out_shape=(jax.ShapeDtyp...]
where the time goes in v5:
time: 99.2 us; the launch traced here: 99 us
  Pallas kernels  98.4 us (99%)
    pallas_call x1, Pallas kernels, on_device(): pl.pallas_call(functools.partial(kernel, n_frame, n_space), out_shape=(ja...  91.7 us
    pallas_call x1, Pallas kernels, on_device(): pl.pallas_call(products, grid=(HEADS // GROUP,), out_shape=(jax.ShapeDtyp...  6.67 us

profile of v5, /device:TPU:0, one launch (start us, length us, event | category | flops | bytes accessed | tf_op | source)
XLA Modules:
  0.0 99.0 jit_solution(6767811812613381982)
XLA Ops:
  0.6 91.7 %shard_map.67 = (f32[20,112,128]{2,1,0:T(8,128)}, f32[20,112,128]{2,1,0:T(8,128)}, bf16[20,128,256]{2,1,0:T(8,128)(2,1)}) custom-call(bf16[20,112,256]{2,1,0:T(8,128)(2,1)} %bitcast.35, bf16[20,112,256]{2,1,0:T(8,128)(2,1)} %bitcast.37, bf16[20,112,256]{2,1,0:T(8,128)(2,1)} %bitcast.39, bf16[20,112,256]{2,1,0:T(8,128)(2,1)} %bitcast.41), custom_call_target="tpu_custom_call" | custom-call | tf_op jit(solution)/shard_map/pallas_call | solution.py:314
  92.4 6.7 %shard_map.68 = (f32[20,112,256]{2,1,0:T(8,128)}, f32[20,112,256]{2,1,0:T(8,128)}, f32[20,112,256]{2,1,0:T(8,128)}) custom-call(f32[20,112,128]{2,1,0:T(8,128)} %get-tuple-element.9.state, f32[20,112,128]{2,1,0:T(8,128)} %get-tuple-element.10.grad, bf16[20,128,256]{2,1,0:T(8,128)(2,1)} %get-tuple-element.11.scaled, bf16[20,112,256]{2,1,0:T(8,128)(2,1)} %bitcast.36, ...), custom_call_target="tpu_custom_call" | custom-call | tf_op jit(solution)/shard_map/pallas_call | solution.py:341

commit v6 on v4

--- a/solution.py
+++ b/solution.py
@@ -12,6 +12,9 @@
 LANES = 128
 LAG = 2
 GROUP = 5
+TILE = 8
+BLOCK = LANES - HEAD_DIM
+BODY = HEAD_DIM - BLOCK
 MESH = pl.DeviceIdType.MESH
 NT = (((1,), (1,)), ((), ()))
 TN = (((0,), (0,)), ((), ()))
@@ -38,6 +41,42 @@
     return functools.reduce(jnp.logical_and, left) if left else True
 
 
+def lanes(rows):
+    return lax.broadcasted_iota(jnp.int32, (rows, LANES), 1)
+
+
+def pack(state, column):
+    bottom, spare = state[BODY:], lanes(BLOCK) >= HEAD_DIM
+    pieces = [
+        jnp.where(spare, pltpu.roll(bottom, HEAD_DIM - at, 1), state[at:at + BLOCK])
+        for at in range(0, BODY, BLOCK)
+    ]
+    lane = lanes(TILE)
+    tail = jnp.where(lane >= HEAD_DIM, pltpu.roll(bottom[:TILE], LANES - HEAD_DIM, 1), bottom[TILE:])
+    for g in range(HEAD_DIM // TILE):
+        tail = jnp.where(lane == g, column[g * TILE:(g + 1) * TILE], tail)
+    return jnp.concatenate(pieces + [tail], axis=0)
+
+
+def unpack(packed, copies):
+    tail, lane = packed[BODY:], lanes(BLOCK)
+    bottom = jnp.concatenate([pltpu.roll(tail, HEAD_DIM, 1), tail], axis=0)
+    pieces = []
+    for at in range(0, BODY, BLOCK):
+        piece = packed[at:at + BLOCK]
+        here = jnp.logical_and(lane >= at, lane < at + BLOCK)
+        bottom = jnp.where(here, pltpu.roll(piece, LANES - HEAD_DIM + at, 1), bottom)
+        pieces.append(piece)
+    pieces.append(bottom)
+    whole = []
+    for i, piece in enumerate(pieces):
+        g = i * BLOCK // TILE
+        column = jnp.concatenate([tail[:, g:g + 1], tail[:, g + 1:g + 2]], axis=0)
+        z = jnp.where(lane < HEAD_DIM + copies, column, 0.0)
+        whole.append(jnp.where(lane < HEAD_DIM, piece, z))
+    return jnp.concatenate(whole, axis=0)
+
+
 def ones_below(tokens):
     row = lax.broadcasted_iota(jnp.int32, (LANES - HEAD_DIM, tokens), 0)
     return row, jnp.where(row < 2, 1.0, 0.0).astype(jnp.bfloat16)
@@ -47,7 +86,7 @@
     n_frame, n_space,
     q_in, k_in, v_in, g_in,
     state_out, grad_out, scaled_out,
-    qs, ks, vs, gs, scaleds,
+    qs, ks, vs, gs, scaleds, plain,
     local, prefix, total, arrived, send_sem, recv_sem, in_sem, out_sem,
 ):
     frame, space = lax.axis_index("frame"), lax.axis_index("space")
@@ -179,13 +218,16 @@
 
     def states(h):
         loaded((0, 1), h)
-        begin(0, h, dot(jnp.maximum(ks[h], 0), values(h), NT))
+        state = dot(jnp.maximum(ks[h], 0), values(h), NT)
+        begin(0, h, pack(state, state[:, HEAD_DIM:HEAD_DIM + 1]))
 
     def queries(h):
         loaded((2, 3), h)
         q = jnp.maximum(qs[h], 0)
+        state = unpack(prefix[0, h], 2)
+        plain[0, h] = state
         store(0, h).start()
-        pair = jnp.concatenate(split(prefix[0, h]), axis=0)
+        pair = jnp.concatenate(split(state), axis=0)
         numerator = dot(pair, jnp.concatenate([q, q], axis=0), TN)
         inverse = 1.0 / (numerator[HEAD_DIM:HEAD_DIM + 1] + 1.0)
         grad = gs[h].astype(jnp.float32)
@@ -193,15 +235,17 @@
         coarse = slope.astype(jnp.bfloat16).astype(jnp.float32)
         slopes = jnp.where(row == 0, coarse, jnp.where(row == 1, slope - coarse, 0.0))
         scaled = jnp.concatenate([grad * inverse, slopes], axis=0).astype(jnp.bfloat16)
-        begin(1, h, dot(q, scaled, NT))
+        grads = dot(q, scaled, NT)
+        begin(1, h, pack(grads, grads[:, HEAD_DIM:HEAD_DIM + 1] + grads[:, HEAD_DIM + 1:HEAD_DIM + 2]))
         scaleds[h] = scaled
         store(2, h).start()
 
     def keys(h):
+        plain[1, h] = unpack(total[1, h], 1)
         store(1, h).start()
 
     def store(i, h):
-        source, target = ((prefix.at[0], state_out), (total.at[1], grad_out), (scaleds, scaled_out))[i]
+        source, target = ((plain.at[0], state_out), (plain.at[1], grad_out), (scaleds, scaled_out))[i]
         return pltpu.make_async_copy(source.at[h], target.at[h], out_sem.at[i, h])
 
     plan = []
@@ -275,6 +319,7 @@
     heads = [jnp.swapaxes(array[0], 0, 1).reshape(HEADS, HEAD_DIM, rows) for array in arrays]
     shape = heads[0].shape
     state = (HEADS, HEAD_DIM, LANES)
+    packed = (HEADS, BODY + TILE, LANES)
     wide = (HEADS, LANES, rows)
     links = (2, levels + 2, HEADS)
     states = pl.pallas_call(
@@ -287,9 +332,9 @@
         in_specs=[pl.BlockSpec(memory_space=pltpu.HBM)] * 4,
         out_specs=(pl.BlockSpec(memory_space=pl.ANY),) * 3,
         scratch_shapes=[pltpu.VMEM(shape, jnp.bfloat16)] * 4 + [pltpu.VMEM(wide, jnp.bfloat16)]
-        + [pltpu.VMEM((2,) + state, jnp.float32)] * 3
+        + [pltpu.VMEM((2,) + state, jnp.float32)] + [pltpu.VMEM((2,) + packed, jnp.float32)] * 3
         + [
-            pltpu.VMEM((2, levels + 2) + state, jnp.float32),
+            pltpu.VMEM((2, levels + 2) + packed, jnp.float32),
             pltpu.SemaphoreType.DMA(links),
             pltpu.SemaphoreType.DMA(links),
             pltpu.SemaphoreType.DMA((4, HEADS // GROUP)),
@@ -308,7 +353,7 @@
         out_shape=(jax.ShapeDtypeStruct(shape, jnp.float32),) * 3,
         in_specs=[some(state), some(state), some(wide)] + [some(shape)] * 3,
         out_specs=(some(shape),) * 3,
-        compiler_params=pltpu.CompilerParams(vmem_limit_bytes=24 * 1024 * 1024),
+        compiler_params=pltpu.CompilerParams(vmem_limit_bytes=56 * 1024 * 1024),
     )(*states, *heads[:3])
     return tuple(jnp.swapaxes(grad.reshape(HEADS * HEAD_DIM, rows), 0, 1)[None] for grad in grads)
 

time: 101 us -> 96.9 us (0.959)
  local copies, waits for them, and re-layouts: 3.84 us -> 0 us
    unnamed x12 -> x0, local copies, waits for them, and re-layouts: 3.84 us -> none
    pallas_call x1, Pallas kernels: 3.73 us -> 6.67 us  [on_device(): pl.pallas_call(products, grid=(HEADS // GROUP,), out_shape=(jax.ShapeDtyp...]
    pallas_call x1, Pallas kernels: 92.3 us -> 89.4 us  [on_device(): pl.pallas_call(functools.partial(kernel, n_frame, n_space), out_shape=(ja...]
where the time goes in v6:
time: 96.9 us; the launch traced here: 96.7 us
  Pallas kernels  96 us (99%)
    pallas_call x1, Pallas kernels, on_device(): pl.pallas_call(functools.partial(kernel, n_frame, n_space), out_shape=(ja...  89.4 us
    pallas_call x1, Pallas kernels, on_device(): pl.pallas_call(products, grid=(HEADS // GROUP,), out_shape=(jax.ShapeDtyp...  6.67 us

profile of v6, /device:TPU:0, one launch (start us, length us, event | category | flops | bytes accessed | tf_op | source)
XLA Modules:
  0.0 96.7 jit_solution(18151987358773650569)
XLA Ops:
  0.6 89.4 %shard_map.67 = (f32[20,112,128]{2,1,0:T(8,128)}, f32[20,112,128]{2,1,0:T(8,128)}, bf16[20,128,256]{2,1,0:T(8,128)(2,1)}) custom-call(bf16[20,112,256]{2,1,0:T(8,128)(2,1)} %bitcast.35, bf16[20,112,256]{2,1,0:T(8,128)(2,1)} %bitcast.37, bf16[20,112,256]{2,1,0:T(8,128)(2,1)} %bitcast.39, bf16[20,112,256]{2,1,0:T(8,128)(2,1)} %bitcast.41), custom_call_target="tpu_custom_call" | custom-call | tf_op jit(solution)/shard_map/pallas_call | solution.py:325
  90.0 6.7 %shard_map.68 = (f32[20,112,256]{2,1,0:T(8,128)}, f32[20,112,256]{2,1,0:T(8,128)}, f32[20,112,256]{2,1,0:T(8,128)}) custom-call(f32[20,112,128]{2,1,0:T(8,128)} %get-tuple-element.9.state, f32[20,112,128]{2,1,0:T(8,128)} %get-tuple-element.10.grad, bf16[20,128,256]{2,1,0:T(8,128)(2,1)} %get-tuple-element.11.scaled, bf16[20,112,256]{2,1,0:T(8,128)(2,1)} %bitcast.36, ...), custom_call_target="tpu_custom_call" | custom-call | tf_op jit(solution)/shard_map/pallas_call | solution.py:350

commit v7 on v6

--- a/solution.py
+++ b/solution.py
@@ -10,7 +10,7 @@
 HEADS = 20
 HEAD_DIM = 112
 LANES = 128
-LAG = 2
+LAG = 3
 GROUP = 5
 TILE = 8
 BLOCK = LANES - HEAD_DIM

time: 96.9 us -> 93.8 us (0.968)
  Pallas kernels: 96 us -> 93 us
    pallas_call x1, Pallas kernels: 89.4 us -> 86.3 us  [on_device(): pl.pallas_call(functools.partial(kernel, n_frame, n_space), out_shape=(ja...]
where the time goes in v7:
time: 93.8 us; the launch traced here: 93.6 us
  Pallas kernels  93 us (99%)
    pallas_call x1, Pallas kernels, on_device(): pl.pallas_call(functools.partial(kernel, n_frame, n_space), out_shape=(ja...  86.3 us
    pallas_call x1, Pallas kernels, on_device(): pl.pallas_call(products, grid=(HEADS // GROUP,), out_shape=(jax.ShapeDtyp...  6.67 us

profile of v7, /device:TPU:0, one launch (start us, length us, event | category | flops | bytes accessed | tf_op | source)
XLA Modules:
  0.0 93.6 jit_solution(13851949135143760775)
XLA Ops:
  0.6 86.3 %shard_map.67 = (f32[20,112,128]{2,1,0:T(8,128)}, f32[20,112,128]{2,1,0:T(8,128)}, bf16[20,128,256]{2,1,0:T(8,128)(2,1)}) custom-call(bf16[20,112,256]{2,1,0:T(8,128)(2,1)} %bitcast.35, bf16[20,112,256]{2,1,0:T(8,128)(2,1)} %bitcast.37, bf16[20,112,256]{2,1,0:T(8,128)(2,1)} %bitcast.39, bf16[20,112,256]{2,1,0:T(8,128)(2,1)} %bitcast.41), custom_call_target="tpu_custom_call" | custom-call | tf_op jit(solution)/shard_map/pallas_call | solution.py:325
  87.0 6.7 %shard_map.68 = (f32[20,112,256]{2,1,0:T(8,128)}, f32[20,112,256]{2,1,0:T(8,128)}, f32[20,112,256]{2,1,0:T(8,128)}) custom-call(f32[20,112,128]{2,1,0:T(8,128)} %get-tuple-element.9.state, f32[20,112,128]{2,1,0:T(8,128)} %get-tuple-element.10.grad, bf16[20,128,256]{2,1,0:T(8,128)(2,1)} %get-tuple-element.11.scaled, bf16[20,112,256]{2,1,0:T(8,128)(2,1)} %bitcast.36, ...), custom_call_target="tpu_custom_call" | custom-call | tf_op jit(solution)/shard_map/pallas_call | solution.py:350

commit v8 on v7

--- a/solution.py
+++ b/solution.py
@@ -252,7 +252,7 @@
 
     def plan_scan(phase, at):
         for level in range(levels):
-            at += LAG
+            at += LAG - 1 if level == 0 else LAG
             plan.insert(0, (at, True, functools.partial(scan_level, phase, level)))
         return at
 

time: 93.8 us -> 92.4 us (0.985)
  Pallas kernels: 93 us -> 91.6 us
    pallas_call x1, Pallas kernels: 86.3 us -> 84.9 us  [on_device(): pl.pallas_call(functools.partial(kernel, n_frame, n_space), out_shape=(ja...]
where the time goes in v8:
time: 92.4 us; the launch traced here: 92.2 us
  Pallas kernels  91.6 us (99%)
    pallas_call x1, Pallas kernels, on_device(): pl.pallas_call(functools.partial(kernel, n_frame, n_space), out_shape=(ja...  84.9 us
    pallas_call x1, Pallas kernels, on_device(): pl.pallas_call(products, grid=(HEADS // GROUP,), out_shape=(jax.ShapeDtyp...  6.67 us

profile of v8, /device:TPU:0, one launch (start us, length us, event | category | flops | bytes accessed | tf_op | source)
XLA Modules:
  0.0 92.2 jit_solution(11085707335216801720)
XLA Ops:
  0.6 84.9 %shard_map.67 = (f32[20,112,128]{2,1,0:T(8,128)}, f32[20,112,128]{2,1,0:T(8,128)}, bf16[20,128,256]{2,1,0:T(8,128)(2,1)}) custom-call(bf16[20,112,256]{2,1,0:T(8,128)(2,1)} %bitcast.35, bf16[20,112,256]{2,1,0:T(8,128)(2,1)} %bitcast.37, bf16[20,112,256]{2,1,0:T(8,128)(2,1)} %bitcast.39, bf16[20,112,256]{2,1,0:T(8,128)(2,1)} %bitcast.41), custom_call_target="tpu_custom_call" | custom-call | tf_op jit(solution)/shard_map/pallas_call | solution.py:325
  85.5 6.7 %shard_map.68 = (f32[20,112,256]{2,1,0:T(8,128)}, f32[20,112,256]{2,1,0:T(8,128)}, f32[20,112,256]{2,1,0:T(8,128)}) custom-call(f32[20,112,128]{2,1,0:T(8,128)} %get-tuple-element.9.state, f32[20,112,128]{2,1,0:T(8,128)} %get-tuple-element.10.grad, bf16[20,128,256]{2,1,0:T(8,128)(2,1)} %get-tuple-element.11.scaled, bf16[20,112,256]{2,1,0:T(8,128)(2,1)} %bitcast.36, ...), custom_call_target="tpu_custom_call" | custom-call | tf_op jit(solution)/shard_map/pallas_call | solution.py:350
